TPU v7x, 128 devices: a whole 4x4x4 slice. The times are simulated.
128 devices in a mesh: blk: 64 (over z_lo, x, y, core), head: 2 (over z_hi).
Axes of the slice: x: 4, y: 4, z: 4 (z_hi: 2, z_lo: 2; z = z_hi * 2 + z_lo), core: 2. Of those that a mesh axis runs over, the one named last changes fastest.
Arguments:
- prefix: bfloat16 [24576, 2048], P(('blk', 'head')), may hold values from -30 to 30
- w_key: bfloat16 [2048, 2048], P(None, 'head'), may hold values from -1 to 1.5
- w_value: bfloat16 [2048, 2048], P(None, 'head'), may hold values from -0.125 to 0.125
- queries: bfloat16 [2048, 2048], P('blk', 'head'), may hold values from -100 to 100
- output_grad: bfloat16 [2048, 2048], P('blk', 'head'), may hold values from -6 to 6
- block_mask: int32 [64, 192], P(None, 'blk'), may hold values from 0 to 1, as said below
Outputs:
- query_grads: bfloat16 [2048, 2048], P('blk', 'head')
- prefix_grads: bfloat16 [24576, 2048], P(('blk', 'head'))
Inputs may be any that keep to these rules, and one draw needn't show every extreme that they name: block_mask[j, c] is 1 where latents j * 32 to (j + 1) * 32 - 1 attend to prefix tokens c * 128 to (c + 1) * 128 - 1, else 0; block_mask[j, j * 3] is 1 for every j.
All inputs are finite; a program needn't handle non-finite values.
Results may differ from a plain program's by a relative error of at most 0.0095.
The roundings to bfloat16 on the way count: a program that leaves them out, or rounds other values in their place, can miss the bound.
Values may be sent and summed in bfloat16 or wider, within the bound.
A program may use at most 128 MiB of HBM per device.

v0:
```python
import math

import jax
import jax.numpy as jnp
from jax import lax
from jax.sharding import PartitionSpec as P

HEAD_DIM = 128
BLOCK = 128


NEG_FILL = -1e30
ROW_LIMIT = 512


def combined_all(part, axis, combine):
    gathered = jax.tree.map(lambda a: lax.all_gather(a, axis), part)

    def take(source):
        return jax.tree.map(lambda a: lax.dynamic_index_in_dim(a, source, 0, False), gathered)

    return lax.fori_loop(
        1, lax.axis_size(axis), lambda source, state: combine(state, take(source)), take(0)
    )


def live_blocks(block_mask, first_row, row_count, shard_rows):
    shard_ids = (first_row + jnp.arange(row_count, dtype=jnp.int32)) // shard_rows
    picked = shard_ids[:, None] == jnp.arange(block_mask.shape[0], dtype=jnp.int32)[None, :]
    return jnp.sum(jnp.where(picked[:, :, None], block_mask[None, :, :], 0), axis=1) > 0


def score_block(query_rows, key_block, score_scale):
    return (
        jnp.einsum("igd,pgd->gip", query_rows, key_block, preferred_element_type=jnp.float32)
        * score_scale
    )


def stats_tile(query_rows, grad_rows, key_block, value_block, live_cells, score_scale):
    scores = jnp.where(live_cells[None], score_block(query_rows, key_block, score_scale), NEG_FILL)
    row_top = jnp.max(scores, axis=2)
    weights = jnp.where(live_cells[None], jnp.exp(scores - row_top[:, :, None]), 0.0)
    output_dots = jnp.einsum(
        "igd,pgd->gip", grad_rows, value_block, preferred_element_type=jnp.float32
    )
    return (row_top, jnp.sum(weights, axis=2), jnp.sum(weights * output_dots, axis=2))


def join_stats(left, right):
    row_top = jnp.maximum(left[0], right[0])
    left_factor = jnp.exp(left[0] - row_top)
    right_factor = jnp.exp(right[0] - row_top)
    return (
        row_top,
        left[1] * left_factor + right[1] * right_factor,
        left[2] * left_factor + right[2] * right_factor,
    )


def grad_tile(
    query_rows, grad_rows, key_block, value_block, live_cells, log_total, row_delta, score_scale
):
    shifted = score_block(query_rows, key_block, score_scale) - log_total[:, :, None]
    attention = jnp.where(live_cells[None], jnp.exp(shifted), 0.0)
    output_dots = jnp.einsum(
        "igd,pgd->gip", grad_rows, value_block, preferred_element_type=jnp.float32
    )
    score_grad = attention * (output_dots - row_delta[:, :, None])
    attention_low = attention.astype(jnp.bfloat16)
    lowered_grad = score_grad.astype(jnp.bfloat16)
    query_grad = (
        jnp.einsum("gip,pgd->igd", lowered_grad, key_block, preferred_element_type=jnp.float32)
        * score_scale
    )
    key_grad = (
        jnp.einsum("gip,igd->pgd", lowered_grad, query_rows, preferred_element_type=jnp.float32)
        * score_scale
    )
    value_grad = jnp.einsum(
        "gip,igd->pgd", attention_low, grad_rows, preferred_element_type=jnp.float32
    )
    return (query_grad, key_grad, value_grad)


def block_stats(query_rows, grad_rows, first_row, context):
    key_heads, value_heads, block_mask, shard_rows, score_scale = context
    blocks = live_blocks(block_mask, first_row, query_rows.shape[0], shard_rows)
    cells = jnp.repeat(blocks, BLOCK, axis=1)
    return stats_tile(query_rows, grad_rows, key_heads, value_heads, cells, score_scale)


def block_grads(query_rows, grad_rows, first_row, log_total, row_delta, context):
    key_heads, value_heads, block_mask, shard_rows, score_scale = context
    blocks = live_blocks(block_mask, first_row, query_rows.shape[0], shard_rows)
    cells = jnp.repeat(blocks, BLOCK, axis=1)
    return grad_tile(
        query_rows, grad_rows, key_heads, value_heads, cells, log_total, row_delta, score_scale
    )


def row_steps(row_count):
    row_block = math.gcd(row_count, ROW_LIMIT)
    return (row_block, row_count // row_block)


def stats_over_rows(whole_stats, query_all, grad_all, context):
    row_block, block_count = row_steps(query_all.shape[0])

    def stats_advance(step_index, totals):
        offset = step_index * row_block
        query_rows = lax.dynamic_slice_in_dim(query_all, offset, row_block, 0)
        grad_rows = lax.dynamic_slice_in_dim(grad_all, offset, row_block, 0)
        tile_part = block_stats(query_rows, grad_rows, offset, context)
        return tuple(
            (
                lax.dynamic_update_slice_in_dim(total_part, new_part, offset, 1)
                for total_part, new_part in zip(totals, tile_part)
            )
        )

    return lax.fori_loop(0, block_count, stats_advance, whole_stats)


def grads_over_rows(totals, query_all, grad_all, log_total, row_delta, context):
    row_block, block_count = row_steps(query_all.shape[0])

    def grads_advance(step_index, running):
        offset = step_index * row_block
        query_rows = lax.dynamic_slice_in_dim(query_all, offset, row_block, 0)
        grad_rows = lax.dynamic_slice_in_dim(grad_all, offset, row_block, 0)
        top_rows = lax.dynamic_slice_in_dim(log_total, offset, row_block, 1)
        delta_rows = lax.dynamic_slice_in_dim(row_delta, offset, row_block, 1)
        query_grad, key_grad, value_grad = block_grads(
            query_rows, grad_rows, offset, top_rows, delta_rows, context
        )
        return (
            running[0] + key_grad,
            running[1] + value_grad,
            lax.dynamic_update_slice_in_dim(running[2], query_grad, offset, 0),
        )

    return lax.fori_loop(0, block_count, grads_advance, totals)


def local(prefix, w_key, w_value, queries, output_grad, block_mask):
    head_cols = w_key.shape[1]
    groups = head_cols // HEAD_DIM
    score_scale = 1.0 / math.sqrt(HEAD_DIM)
    shard_rows = queries.shape[0]
    latents = shard_rows * lax.axis_size("blk")
    slab_rows = lax.all_gather(prefix, "head", axis=0, tiled=True)
    key_part = jnp.dot(slab_rows, w_key, preferred_element_type=jnp.float32).astype(jnp.bfloat16)
    value_part = jnp.dot(slab_rows, w_value, preferred_element_type=jnp.float32).astype(
        jnp.bfloat16
    )
    projected = jnp.stack((key_part, value_part), axis=0)
    prefix_len = projected.shape[1]
    key_heads = projected[0].reshape(prefix_len, groups, HEAD_DIM)
    value_heads = projected[1].reshape(prefix_len, groups, HEAD_DIM)
    context = (key_heads, value_heads, block_mask, shard_rows, score_scale)
    stat_shape = (groups, latents)
    stats_start = (
        jnp.full(stat_shape, NEG_FILL, jnp.float32),
        jnp.zeros(stat_shape, jnp.float32),
        jnp.zeros(stat_shape, jnp.float32),
    )
    query_all, grad_all = (
        lax.all_gather(queries, "blk", axis=0, tiled=True),
        lax.all_gather(output_grad, "blk", axis=0, tiled=True),
    )
    query_all = query_all.reshape(latents, groups, HEAD_DIM)
    grad_all = grad_all.reshape(latents, groups, HEAD_DIM)
    local_stats = stats_over_rows(stats_start, query_all, grad_all, context)
    row_top, row_total, row_inner = combined_all(
        (local_stats[0], local_stats[1], local_stats[2]), "blk", join_stats
    )
    log_total = row_top + jnp.log(row_total)
    row_delta = row_inner / row_total
    grads_start = (
        jnp.zeros((prefix_len, groups, HEAD_DIM), jnp.float32),
        jnp.zeros((prefix_len, groups, HEAD_DIM), jnp.float32),
        jnp.zeros((latents, groups, HEAD_DIM), jnp.float32),
    )
    key_sum, value_sum, query_sum = grads_over_rows(
        grads_start, query_all, grad_all, log_total, row_delta, context
    )
    query_grads = lax.psum_scatter(
        query_sum.reshape(latents, head_cols), "blk", scatter_dimension=0, tiled=True
    ).astype(jnp.bfloat16)
    key_grads = key_sum.astype(jnp.bfloat16).reshape(prefix_len, head_cols)
    value_grads = value_sum.astype(jnp.bfloat16).reshape(prefix_len, head_cols)
    contract = (((1,), (1,)), ((), ()))
    back_keys = lax.dot_general(key_grads, w_key, contract, preferred_element_type=jnp.float32)
    prefix_grads = lax.psum_scatter(
        back_keys
        + lax.dot_general(value_grads, w_value, contract, preferred_element_type=jnp.float32),
        "head",
        scatter_dimension=0,
        tiled=True,
    ).astype(jnp.bfloat16)
    return (query_grads, prefix_grads)


def solution(mesh):
    return jax.shard_map(
        local,
        mesh=mesh,
        in_specs=(
            P(("blk", "head"), None),
            P(None, "head"),
            P(None, "head"),
            P("blk", "head"),
            P("blk", "head"),
            P(None, "blk"),
        ),
        out_specs=(P("blk", "head"), P(("blk", "head"), None)),
        check_vma=False,
    )
```

profile of v0, /device:TPU:0, one launch (start us, length us, event | category | flops | bytes accessed | tf_op | source)
XLA Modules:
  0.0 1167.3 jit_solution(8079495356362397994)
XLA Ops:
  9.4 34.1 %all-gather.12.cloned.1.call-done = bf16[384,2048]{1,0:T(8,128)(2,1)} async-done(((bf16[192,2048]{1,0:T(8,128)(2,1)}), bf16[384,2048]{1,0:T(8,128)(2,1)}) %all-gather.12.cloned.1.call-update) | async-done | bytes 1572880 | tf_op jit(solution)/shard_map/all_gather | solution.py:152
  43.6 4.6 fusion.37
  48.2 1.8 fusion.36
  50.4 100.0 %all-gather.10.cloned.1.call-done = bf16[2048,1024]{1,0:T(8,128)(2,1)} async-done(((bf16[32,1024]{1,0:T(8,128)(2,1)}), bf16[2048,1024]{1,0:T(8,128)(2,1)}) %all-gather.10.cloned.1.call-update) | async-done | bytes 4194320 | tf_op jit(solution)/shard_map/all_gather | solution.py:169
  150.4 6.5 copy.52
  156.9 6.5 copy.58
  163.4 93.6 %all-gather.14.cloned.1.call-done = bf16[2048,1024]{1,0:T(8,128)(2,1)} async-done(((bf16[32,1024]{1,0:T(8,128)(2,1)}), bf16[2048,1024]{1,0:T(8,128)(2,1)}) %all-gather.14.cloned.1.call-update) | async-done | bytes 4194320 | tf_op jit(solution)/shard_map/all_gather | solution.py:170
  257.0 6.6 copy.53
  263.6 6.5 copy.56
  270.1 30.8 %while.58 = (s32[]{:T(128)}, f32[8,2048]{1,0:T(8,128)S(1)}, f32[8,2048]{1,0:T(8,128)S(1)}, f32[8,2048]{1,0:T(8,128)S(1)}, s32[64,3]{0,1:T(4,128)S(1)}, /*index=5...) while((s32[]{:T(128)}, f32[8,2048]{1,0:T(8,128)S(1)}, ...), condition=%wide.region_5.6_spmd, body=%wide.region_0.5_spmd.sunk | while | flops 827551744 | bytes 23596992 | solution.py:122
  270.4 2.4 fusion.76
  272.8 3.5 multiply_reduce_fusion.2
  276.2 1.5 fusion.77
  278.1 2.4 fusion.76
  280.5 3.5 multiply_reduce_fusion.2
  283.9 1.5 fusion.77
  285.8 2.4 fusion.76
  288.2 3.5 multiply_reduce_fusion.2
  291.6 1.5 fusion.77
  293.5 2.4 fusion.76
  295.9 3.5 multiply_reduce_fusion.2
  299.3 1.5 fusion.77
  303.0 103.7 %all-gather.18.cloned.1.call-done = f32[512,2048]{1,0:T(8,128)} async-done(((f32[8,2048]{1,0:T(8,128)}), f32[512,2048]{1,0:T(8,128)}) %all-gather.18.cloned.1.call-update) | async-done | bytes 4194320 | tf_op jit(solution)/shard_map/all_gather | solution.py:17
  407.6 106.3 %all-gather.16.cloned.1.call-done = f32[512,2048]{1,0:T(8,128)} async-done(((f32[8,2048]{1,0:T(8,128)}), f32[512,2048]{1,0:T(8,128)}) %all-gather.16.cloned.1.call-update) | async-done | bytes 4194320 | tf_op jit(solution)/shard_map/all_gather | solution.py:17
  514.7 105.7 %all-gather.20.cloned.1.call-done = f32[512,2048]{1,0:T(8,128)} async-done(((f32[8,2048]{1,0:T(8,128)}), f32[512,2048]{1,0:T(8,128)}) %all-gather.20.cloned.1.call-update) | async-done | bytes 4194320 | tf_op jit(solution)/shard_map/all_gather | solution.py:17
  621.2 118.5 %while.59 = (s32[]{:T(128)}, f32[8,2048]{1,0:T(8,128)S(1)}, f32[8,2048]{1,0:T(8,128)S(1)}, f32[8,2048]{1,0:T(8,128)S(1)}, f32[64,8,2048]{2,1,0:T(8,128)}, /*inde...) while((s32[]{:T(128)}, f32[8,2048]{1,0:T(8,128)S(1)}, ...), condition=%wide.region_7.8_spmd, body=%wide.region_6.7_spmd.sunk | while | flops 180229 | bytes 917647 | solution.py:22
  644.7 0.9 fusion.79
  646.6 0.9 fusion.79
  680.4 0.9 fusion.79
  682.3 0.9 fusion.79
  739.7 3.6 broadcast_in_dim.239.clone
  743.3 60.9 %while.60 = (s32[]{:T(128)}, f32[384,8,128]{0,2,1:T(8,128)S(1)}, f32[384,8,128]{0,2,1:T(8,128)}, f32[2048,8,128]{2,1,0:T(8,128)}, bf16[2048,8,128]{2,0,1:T(8,128...) while((s32[]{:T(128)}, f32[384,8,128]{0,2,1:T(8,128)S(1)}, ...), condition=%wide.region_10.11_spmd.clone, body=%wide.region_8.10_spmd.clone.sunk | while | flops 2031722496 | bytes 79112456 | solution.py:143
  744.5 2.4 fusion.90
  747.5 2.3 bitcast_add_fusion.5
  749.8 2.7 multiply_convert_fusion.2
  752.6 2.3 bitcast_add_fusion.4
  754.9 1.0 multiply_bitcast_fusion.2
  755.9 2.6 copy_dynamic-update-slice_fusion.2
  759.8 2.4 fusion.90
  762.7 2.3 bitcast_add_fusion.5
  765.1 2.7 multiply_convert_fusion.2
  767.8 2.3 bitcast_add_fusion.4
  770.2 1.0 multiply_bitcast_fusion.2
  771.2 2.5 copy_dynamic-update-slice_fusion.2
  775.0 2.4 fusion.90
  777.9 2.3 bitcast_add_fusion.5
  780.3 2.7 multiply_convert_fusion.2
  783.0 2.3 bitcast_add_fusion.4
  785.3 1.0 multiply_bitcast_fusion.2
  786.3 2.6 copy_dynamic-update-slice_fusion.2
  790.2 2.4 fusion.90
  793.2 2.3 bitcast_add_fusion.5
  795.5 2.7 multiply_convert_fusion.2
  798.2 2.3 bitcast_add_fusion.4
  800.6 1.0 multiply_bitcast_fusion.2
  801.6 2.6 copy_dynamic-update-slice_fusion.2
  804.3 1.7 convert_element_type.42
  806.9 1.9 fusion.39
  809.1 3.5 convolution_add_fusion
  812.8 9.3 copy.74
  822.2 37.1 %reduce-scatter.5.cloned.1.call-done = f32[192,2048]{1,0:T(8,128)} async-done(((f32[384,2048]{1,0:T(8,128)}), f32[192,2048]{1,0:T(8,128)}) %reduce-scatter.5.cloned.1.call-update) | async-done | bytes 1572880 | tf_op jit(solution)/shard_map/reduce_scatter | solution.py:195
  859.3 2.4 convert_element_type.43
  861.7 297.3 %reduce-scatter.3.cloned.1.call-done = f32[32,1024]{1,0:T(8,128)} async-done(((f32[2048,1024]{1,0:T(8,128)}), f32[32,1024]{1,0:T(8,128)}) %reduce-scatter.3.cloned.1.call-update) | async-done | bytes 131088 | tf_op jit(solution)/shard_map/reduce_scatter | solution.py:188
  1158.9 1.5 convert_element_type.40
  (364 shorter events, 129.8 us)
Async XLA Ops:
  7.2 36.4 %all-gather.12.cloned.1.call-start = ((), (), s32[]{:S(2)}) async-start(), calls=%async_computation.3 | async-start | bytes 2359296 | tf_op jit(solution)/shard_map/all_gather | solution.py:152
  7.9 142.5 %all-gather.10.cloned.1.call-start = ((), (), s32[]{:S(2)}) async-start(), calls=%async_computation.2 | async-start | bytes 4259840 | tf_op jit(solution)/shard_map/all_gather | solution.py:169
  8.6 248.4 %all-gather.14.cloned.1.call-start = ((), (), s32[]{:S(2)}) async-start(), calls=%async_computation.4 | async-start | bytes 4259840 | tf_op jit(solution)/shard_map/all_gather | solution.py:170
  9.4 397.3 %all-gather.18.cloned.1.call-start = ((), (), s32[]{:S(2)}) async-start(), calls=%async_computation.8 | async-start | bytes 4259840 | tf_op jit(solution)/shard_map/all_gather | solution.py:17
  43.5 4.6 copy-start.14
  43.6 4.6 copy-start.17
  263.6 6.5 copy-start.11
  300.9 0.6 copy-start.9
  300.9 0.7 copy-start.10
  300.9 1.3 copy-start.8
  301.6 212.3 %all-gather.16.cloned.1.call-start = ((), (), s32[]{:S(2)}) async-start(), calls=%async_computation.7 | async-start | bytes 4259840 | tf_op jit(solution)/shard_map/all_gather | solution.py:17
  302.1 318.2 %all-gather.20.cloned.1.call-start = ((), (), s32[]{:S(2)}) async-start(), calls=%async_computation.9 | async-start | bytes 4259840 | tf_op jit(solution)/shard_map/all_gather | solution.py:17
  302.7 556.5 %reduce-scatter.5.cloned.1.call-start = ((), (), s32[]{:S(2)}) async-start(), calls=%async_computation.6 | async-start | bytes 4718592 | tf_op jit(solution)/shard_map/reduce_scatter | solution.py:195
  743.3 0.8 copy-start.4
  743.3 0.9 copy-start.6
  743.3 0.9 copy-start.12
  744.5 2.5 copy-start
  744.5 3.0 copy-start.1
  744.5 3.0 copy-start.3
  749.8 2.7 copy-start.2
  754.9 3.6 copy-start.5
  754.9 3.6 copy-start.7
  754.9 3.6 copy-start.13
  758.5 0.9 copy-start.4
  758.5 0.9 copy-start.6
  758.5 0.9 copy-start.12
  759.7 2.5 copy-start
  759.7 3.0 copy-start.1
  759.8 3.0 copy-start.3
  765.1 2.7 copy-start.2
  770.1 3.6 copy-start.5
  770.1 3.5 copy-start.7
  770.1 3.5 copy-start.13
  773.7 0.9 copy-start.4
  773.7 0.9 copy-start.6
  773.7 0.9 copy-start.12
  774.9 2.5 copy-start
  774.9 3.0 copy-start.1
  774.9 3.0 copy-start.3
  780.3 2.7 copy-start.2
  785.3 3.6 copy-start.5
  785.3 3.6 copy-start.7
  785.3 3.6 copy-start.13
  788.9 0.9 copy-start.4
  788.9 0.9 copy-start.6
  789.0 0.9 copy-start.12
  790.2 2.5 copy-start
  790.2 3.0 copy-start.1
  790.2 3.0 copy-start.3
  795.5 2.7 copy-start.2
  800.6 3.7 copy-start.5
  800.6 3.6 copy-start.7
  800.6 3.6 copy-start.13
  804.2 2.7 copy-start.15
  806.9 2.2 copy-start.16
  812.6 346.4 %reduce-scatter.3.cloned.1.call-start = ((), (), s32[]{:S(2)}) async-start(), calls=%async_computation.5 | async-start | bytes 8519680 | tf_op jit(solution)/shard_map/reduce_scatter | solution.py:188
Sparse Core Ops, SparseCore 0:
  9.6 33.8 all-gather.11
  45.3 105.0 all-gather.9
  152.1 104.8 all-gather.13
  301.7 104.9 all-gather.17
  408.8 104.9 all-gather.15
  515.4 104.9 all-gather.19
  812.7 46.5 reduce-scatter.4
  861.8 297.1 reduce-scatter.2
where the time goes:
time: 1170 us
  waiting for transfers between devices  881 us (75%)
  other arithmetic  129 us (11%)
  matrix products  78 us (7%)
  local copies, waits for them, and re-layouts  61.2 us (5%)
  between operations  14.3 us (1%)
    all_gather x3, waiting for transfers between devices, combined_all(): gathered = jax.tree.map(lambda a: lax.all_gather(a, axis), part)  316 us
    reduce_scatter x1, waiting for transfers between devices, local(): lax.psum_scatter(query_sum.reshape(latents, head_cols), 'blk', scatter_di...  297 us
    all_gather x1, waiting for transfers between devices, local(): lax.all_gather(queries, 'blk', axis=0, tiled=True)  100 us
    all_gather x1, waiting for transfers between devices, local(): lax.all_gather(output_grad, 'blk', axis=0, tiled=True)  93.6 us
    add x63, other arithmetic, join_stats(): left[1] * left_factor + right[1] * right_factor  58.4 us
    add x63, other arithmetic, join_stats(): left[2] * left_factor + right[2] * right_factor  58 us
    reduce_scatter x1, waiting for transfers between devices, local(): lax.psum_scatter(back_keys + lax.dot_general(value_grads, w_value, contra...  37.1 us
    all_gather x1, waiting for transfers between devices, local(): slab_rows = lax.all_gather(prefix, 'head', axis=0, tiled=True)  34.1 us
  transfers between devices with their start and end apart: 8, of which 8 were waited for; matrix products, arithmetic and copies ran while one was open for 3% of the time, Pallas kernels for 0%

commit v1 on v0

v1 whole, which is shorter than its diff:
```python
import math

import jax
import jax.numpy as jnp
from jax import lax
from jax.experimental import pallas as pl
from jax.experimental.pallas import tpu as pltpu
from jax.sharding import PartitionSpec as P

MESH = pl.DeviceIdType.MESH
HEAD_DIM = 128
BLOCK = 128
UNIT = 64
FILL = -1e30
F32 = jnp.float32
BF16 = jnp.bfloat16

NZ, NX, NY = 2, 4, 4
PEERS = NZ * NX * NY
HEADS = 8
LAT = 32
ROWS = 192
COLS = HEADS * HEAD_DIM
D = 2048
LATENTS = PEERS * LAT
TILE = 256
TILES = LATENTS // TILE
STEPS = HEADS * TILES
LAG = 4
CHUNKS = 2
GROUPS = 4
SCALE = 1.0 / math.sqrt(HEAD_DIM)
SCALE2 = SCALE * math.log2(math.e)
NT = (((1,), (1,)), ((), ()))
TN = (((0,), (0,)), ((), ()))
NN = (((1,), (0,)), ((), ()))


def dot(a, b, dims):
    return lax.dot_general(a, b, dims, preferred_element_type=F32)


def lanes(index, width):
    return pl.ds(pl.multiple_of(index * width, width), width)


def kernel(
    prefix, w_key, w_value, queries, grads, mask,
    dq_out, pg_out,
    w, pref, gat, kv, mask_in, bias, stat, stat_in, glob, p_low, s_low, dq, r1, r2, r3, r4, r5,
    dkv, dkv_in, low, back, back_in,
    w_sem, own_sem, send_sem, recv_sem, stat_send, stat_recv, glob_send, glob_recv,
    dkv_send, dkv_recv, back_send, back_recv,
):
    b = lax.axis_index("blk")
    head = lax.axis_index("head")
    core = lax.rem(b, 2)
    me = lax.div(b, 2)
    y = lax.rem(me, NY)
    x = lax.rem(lax.div(me, NY), NX)
    z = lax.div(me, NX * NY)

    def peer(index):
        return (2 * index + core, head)

    def at(z_, x_, y_):
        return peer((z_ * NX + x_) * NY + y_)

    up = lambda v, k: lax.rem(v + k, 4)
    x1, x2, x3 = up(x, 1), up(x, 2), up(x, 3)
    y1, y2, y3 = up(y, 1), up(y, 2), up(y, 3)
    xp, xm, yp, ym, zn = at(z, x1, y), at(z, x3, y), at(z, x, y1), at(z, x, y3), at(1 - z, x, y)
    sibling = (2 * me + 1 - core, head)
    partner = (b, 1 - head)

    barrier = pltpu.get_barrier_semaphore()

    def greet(k, carry):
        pl.semaphore_signal(
            barrier, inc=1, device_id=peer(lax.rem(me + k, PEERS)), device_id_type=MESH
        )
        return carry

    lax.fori_loop(1, PEERS, greet, 0)
    pl.semaphore_signal(barrier, inc=1, device_id=sibling, device_id_type=MESH)
    pl.semaphore_signal(barrier, inc=1, device_id=partner, device_id_type=MESH)

    w_copies = [
        pltpu.make_async_copy(w_key, w.at[0], w_sem.at[0]),
        pltpu.make_async_copy(w_value, w.at[1], w_sem.at[1]),
    ]
    for copy in w_copies:
        copy.start()
    pl.semaphore_wait(barrier, PEERS + 1)

    used = []

    def send(src, dst, device):
        index = len(used)
        copy = pltpu.make_async_remote_copy(
            src_ref=src, dst_ref=dst, send_sem=send_sem.at[index], recv_sem=recv_sem.at[index],
            device_id=device, device_id_type=MESH,
        )
        copy.start()
        used.append(copy)
        return copy

    shards = (queries, grads)
    rings = (((xp, xm, x, x1, x3), (yp, ym, y, y1, y3)), ((yp, ym, y, y1, y3), (xp, xm, x, x1, x3)))

    def block(t, z_, first, second, cols):
        if t == 0:
            return gat.at[0, z_, first, second, :, cols]
        return gat.at[1, z_, second, first, :, cols]

    def line(t, z_, second, cols):
        if t == 0:
            return gat.at[0, z_, :, second, :, cols]
        return gat.at[1, z_, second, :, :, cols]

    width = COLS // CHUNKS
    flight = {}

    def relay(c, step):
        cols = pl.ds(c * width, width)
        for t in range(2):
            (p1, m1, a, a_up, a_dn), (p2, m2, e, e_up, e_dn) = rings[t]
            key = (c, t)
            if step == 0:
                mine = shards[t].at[:, cols]
                dst = block(t, z, a, e, cols)
                own = pltpu.make_async_copy(mine, dst, own_sem.at[2 * c + t])
                own.start()
                flight[key] = [send(mine, dst, zn), send(mine, dst, p1), send(mine, dst, m1), own]
            elif step == 1:
                flight[key][0].wait_recv()
                src = block(t, 1 - z, a, e, cols)
                flight[key] += [send(src, src, p1), send(src, src, m1)]
            elif step == 2:
                for k in (1, 2, 4, 5):
                    flight[key][k].wait_recv()
                flight[key][3].wait()
                lo, hi = block(t, 0, a_dn, e, cols), block(t, 1, a_up, e, cols)
                flight[key] = [send(lo, lo, p1), send(hi, hi, m1)]
            elif step == 3:
                for k in (0, 1):
                    flight[key][k].wait_recv()
                flight[key] = []
                for z_ in range(NZ):
                    src = line(t, z_, e, cols)
                    flight[key] += [send(src, src, p2), send(src, src, m2)]
            elif step == 4:
                for k in range(4):
                    flight[key][k].wait_recv()
                lo, hi = line(t, 0, e_dn, cols), line(t, 1, e_up, cols)
                flight[key] = [send(lo, lo, p2), send(hi, hi, m2)]
            else:
                for k in (0, 1):
                    flight[key][k].wait_recv()

    for c in range(CHUNKS):
        relay(c, 0)
    pref_copy = send(prefix, pref, partner)
    mask_copy = send(mask.at[1 - core], mask_in, sibling)

    def project(rows, half):
        def column(j, carry):
            for i in range(2):
                cols = lanes(j, 256)
                kv[i, core, half, :, cols] = dot(rows[...], w[i, :, cols], NN).astype(BF16)
            return carry

        lax.fori_loop(0, COLS // 256, column, 0)
        return [send(kv.at[i, core, half], kv.at[i, core, half], sibling) for i in range(2)]

    relay(0, 1)
    relay(1, 1)
    for copy in w_copies:
        copy.wait()
    kv_copies = project(prefix, head)
    relay(0, 2)
    relay(1, 2)

    which = lax.broadcasted_iota(jnp.int32, (BLOCK, LATENTS), 0)
    latent = lax.broadcasted_iota(jnp.int32, (BLOCK, LATENTS), 1)
    spread = jnp.where(lax.div(latent, LAT) == which, 1.0, 0.0).astype(BF16)

    def fill_bias(row_core, source):
        for half in range(2):
            live = dot(source[half].astype(BF16), spread, NN)
            bias[row_core, half] = jnp.where(live > 0.5, 0.0, FILL)

    fill_bias(core, mask[core])
    mask_copy.wait_recv()
    fill_bias(1 - core, mask_in[...])
    relay(0, 3)
    relay(1, 3)
    pref_copy.wait_recv()
    kv_copies += project(pref, 1 - head)
    relay(0, 4)
    relay(1, 4)
    relay(0, 5)
    relay(1, 5)
    for copy in kv_copies:
        copy.wait_recv()

    def stat_copy(step):
        return pltpu.make_async_remote_copy(
            src_ref=stat.at[step], dst_ref=stat_in.at[me],
            send_sem=stat_send.at[step], recv_sem=stat_recv.at[me],
            device_id=peer(step), device_id_type=MESH,
        )

    def glob_copy(k):
        target = lax.rem(me + k, PEERS)
        return pltpu.make_async_remote_copy(
            src_ref=glob.at[me], dst_ref=glob.at[me],
            send_sem=glob_send.at[k], recv_sem=glob_recv.at[me],
            device_id=peer(target), device_id_type=MESH,
        )

    def stat_arrival(j):
        return pltpu.make_async_remote_copy(
            src_ref=stat.at[j], dst_ref=stat_in.at[j],
            send_sem=stat_send.at[j], recv_sem=stat_recv.at[j],
            device_id=peer(j), device_id_type=MESH,
        )

    def glob_arrival(j):
        return pltpu.make_async_remote_copy(
            src_ref=glob.at[j], dst_ref=glob.at[j],
            send_sem=glob_send.at[0], recv_sem=glob_recv.at[j],
            device_id=peer(j), device_id_type=MESH,
        )

    def join():
        def arrive(k, carry):
            stat_arrival(lax.rem(me + k, PEERS)).wait_recv()
            return carry

        lax.fori_loop(1, PEERS, arrive, 0)
        stat_in[me] = stat[me]
        tops = [stat_in[j, 0:1, :] for j in range(PEERS)]
        top = tops[0]
        for j in range(1, PEERS):
            top = jnp.maximum(top, tops[j])
        total = jnp.zeros_like(top)
        inner = jnp.zeros_like(top)
        for j in range(PEERS):
            factor = jnp.exp2(tops[j] - top)
            total += stat_in[j, 1:2, :] * factor
            inner += stat_in[j, 2:3, :] * factor
        glob[me, 0:1, :] = top + jnp.log2(total)
        glob[me, 1:2, :] = inner / total

        def spread_out(k, carry):
            glob_copy(k).start()
            return carry

        lax.fori_loop(1, PEERS, spread_out, 0)

    def latent_rows(t, n, cols):
        rows = gat[t, lax.div(n, 2), pl.ds(2 * lax.rem(n, 2), 2), :, :, cols]
        return rows.reshape(TILE, HEAD_DIM)

    def forward(step, carry):
        h = lax.div(step, TILES)
        n = lax.rem(step, TILES)
        cols = lanes(h, HEAD_DIM)
        where = lanes(n, TILE)
        key = kv[0, :, :, :, cols].reshape(4 * ROWS, HEAD_DIM)
        value = kv[1, :, :, :, cols].reshape(4 * ROWS, HEAD_DIM)
        scores = dot(key, latent_rows(0, n, cols), NT)
        dots = dot(value, latent_rows(1, n, cols), NT)
        parts = []
        top = None
        for u in range(4 * ROWS // UNIT):
            row = bias[u // 6, (u // 3) % 2, u % 3 : u % 3 + 1, where]
            part = scores[u * UNIT : (u + 1) * UNIT] * SCALE2 + row
            parts.append(part)
            top = part if top is None else jnp.maximum(top, part)
        top = jnp.max(top, axis=0, keepdims=True)
        total = inner = None
        for u, part in enumerate(parts):
            weight = jnp.exp2(part - top)
            term = weight * dots[u * UNIT : (u + 1) * UNIT]
            total = weight if total is None else total + weight
            inner = term if inner is None else inner + term
        stat[step, 0:1, :] = top
        stat[step, 1:2, :] = jnp.sum(total, axis=0, keepdims=True)
        stat[step, 2:3, :] = jnp.sum(inner, axis=0, keepdims=True)

        @pl.when(step != me)
        def _():
            stat_copy(step).start()

        @pl.when(step == me + LAG)
        def _():
            join()

        return carry

    stat[...] = jnp.zeros_like(stat)
    glob[...] = jnp.zeros_like(glob)
    lax.fori_loop(0, STEPS, forward, 0)

    def backward(part, half, h):
        cols = lanes(h, HEAD_DIM)
        key = kv[0, :, half, :, cols].reshape(2 * ROWS, HEAD_DIM)
        value = kv[1, :, half, :, cols].reshape(2 * ROWS, HEAD_DIM)
        for n in range(TILES):
            step = h * TILES + n
            if part == 0:

                @pl.when(step + STEPS == me + LAG)
                def _():
                    join()

                @pl.when(step != me)
                def _():
                    glob_arrival(step).wait_recv()

            where = pl.ds(n * TILE, TILE)
            query = latent_rows(0, n, cols)
            grad = latent_rows(1, n, cols)
            scores = dot(key, query, NT)
            dots = dot(value, grad, NT)
            total = glob[step, 0:1, :]
            delta = glob[step, 1:2, :]
            for u in range(2 * ROWS // UNIT):
                rows = pl.ds(u * UNIT, UNIT)
                shift = bias[u // 3, half, u % 3 : u % 3 + 1, where] - total
                weight = jnp.exp2(scores[u * UNIT : (u + 1) * UNIT] * SCALE2 + shift)
                change = weight * (dots[u * UNIT : (u + 1) * UNIT] - delta)
                p_low[rows, where] = weight.astype(BF16)
                s_low[rows, where] = change.astype(BF16)
        query = gat[0, :, :, :, :, cols].reshape(LATENTS, HEAD_DIM)
        grad = gat[1, :, :, :, :, cols].reshape(LATENTS, HEAD_DIM)
        change = s_low[...]
        dkv[part, 0, :, :, cols] = dot(change, query, NN).reshape(2, ROWS, HEAD_DIM)
        dkv[part, 1, :, :, cols] = dot(p_low[...], grad, NN).reshape(2, ROWS, HEAD_DIM)
        query_grad = dot(change, key, TN).reshape(NZ, NX, NY, LAT, HEAD_DIM)
        if part == 0:
            dq[h] = query_grad
        else:
            dq[h] = dq[h] + query_grad
        dkv_copy(part, h).start()

    def dkv_copy(part, h):
        cols = lanes(h, HEAD_DIM)
        return pltpu.make_async_remote_copy(
            src_ref=dkv.at[part, :, 1 - core, :, cols], dst_ref=dkv_in.at[part, :, :, cols],
            send_sem=dkv_send.at[part, h], recv_sem=dkv_recv.at[part, h],
            device_id=sibling, device_id_type=MESH,
        )

    def lower(part):
        def arrive(h, carry):
            dkv_copy(part, h).wait_recv()
            return carry

        lax.fori_loop(0, HEADS, arrive, 0)
        low[0] = ((dkv[part, 0, core] + dkv_in[part, 0]) * SCALE).astype(BF16)
        low[1] = (dkv[part, 1, core] + dkv_in[part, 1]).astype(BF16)

    def back_product(j):
        rows = lanes(j, 256)
        return dot(low[0], w[0, rows, :], NT) + dot(low[1], w[1, rows, :], NT)

    def back_copy(j):
        cols = lanes(j, 256)
        return pltpu.make_async_remote_copy(
            src_ref=back.at[:, cols], dst_ref=back_in.at[:, cols],
            send_sem=back_send.at[j], recv_sem=back_recv.at[j],
            device_id=partner, device_id_type=MESH,
        )

    def first_part(h, carry):
        backward(0, 1 - head, h)
        return carry

    def second_part(h, carry):
        backward(1, head, h)
        return carry

    lax.fori_loop(0, HEADS, first_part, 0)
    lower(0)

    def back_send_out(j, carry):
        back[:, lanes(j, 256)] = back_product(j)
        back_copy(j).start()
        return carry

    lax.fori_loop(0, D // 256, back_send_out, 0)
    lax.fori_loop(0, HEADS, second_part, 0)

    size = HEADS // GROUPS
    ahead = {}

    def reduce(g, step):
        hs = pl.ds(g * size, size)
        first, second = rings[1 - g % 2]
        (p1, m1, a, a1, a3), (p2, m2, e, e1, e3) = first, second
        a2, e2 = up(a, 2), up(e, 2)

        def plane(z_, k):
            return dq.at[hs, z_, :, k] if g % 2 == 0 else dq.at[hs, z_, k]

        def planes(k):
            return dq.at[hs, :, :, k] if g % 2 == 0 else dq.at[hs, :, k]

        def cell(z_, k):
            return dq.at[hs, z_, k, a] if g % 2 == 0 else dq.at[hs, z_, a, k]

        def cells(k):
            return dq.at[hs, :, k, a] if g % 2 == 0 else dq.at[hs, :, a, k]

        def add(ref, *terms):
            value = ref[...]
            for term in terms:
                value = value + term
            ref[...] = value

        if step == 0:
            ahead[g] = [send(plane(0, a2), r1.at[g, 0], p1), send(plane(1, a2), r1.at[g, 1], m1)]
            return
        for copy in ahead[g]:
            copy.wait_recv()
        if step == 1:
            add(plane(0, a1), r1[g, 0])
            add(plane(1, a3), r1[g, 1])
            ahead[g] = [send(planes(a1), r2.at[g, 0], p1), send(planes(a3), r2.at[g, 1], m1)]
        elif step == 2:
            add(planes(a), r2[g, 0], r2[g, 1])
            ahead[g] = [send(cell(0, e2), r3.at[g, 0], p2), send(cell(1, e2), r3.at[g, 1], m2)]
        elif step == 3:
            add(cell(0, e1), r3[g, 0])
            add(cell(1, e3), r3[g, 1])
            ahead[g] = [send(cells(e1), r4.at[g, 0], p2), send(cells(e3), r4.at[g, 1], m2)]
        elif step == 4:
            add(cells(e), r4[g, 0], r4[g, 1])
            ahead[g] = [send(dq.at[hs, 1 - z, x, y], r5.at[g], zn)]
        else:
            result = ((dq[hs, z, x, y] + r5[g]) * SCALE).astype(BF16)
            for k in range(size):
                dq_out[:, pl.ds((g * size + k) * HEAD_DIM, HEAD_DIM)] = result[k]

    pairs = GROUPS // 2
    for wave in range(6 + pairs - 1):
        for g in range(GROUPS):
            if 0 <= wave - g // 2 < 6:
                reduce(g, wave - g // 2)

    lower(1)

    def finish(j, carry):
        cols = lanes(j, 256)
        mine = back_product(j)
        back_copy(j).wait_recv()
        pg_out[:, cols] = (mine + back_in[:, cols]).astype(BF16)
        return carry

    lax.fori_loop(0, D // 256, finish, 0)

    for copy in used:
        copy.wait_send()

    def settle(k, carry):
        stat_copy(lax.rem(me + k, PEERS)).wait_send()
        glob_copy(k).wait_send()
        return carry

    lax.fori_loop(1, PEERS, settle, 0)

    def settle_heads(h, carry):
        dkv_copy(0, h).wait_send()
        dkv_copy(1, h).wait_send()
        back_copy(h).wait_send()
        return carry

    lax.fori_loop(0, HEADS, settle_heads, 0)


def local(prefix, w_key, w_value, queries, output_grad, block_mask):
    live = (block_mask != 0).astype(F32).reshape(PEERS, 2, 3).transpose(1, 2, 0)
    units = jnp.repeat(live, BLOCK // UNIT, axis=1).reshape(2, 2, 3, PEERS)
    mask = jnp.pad(units, ((0, 0), (0, 0), (0, 5), (0, BLOCK - PEERS)))
    size = HEADS // GROUPS
    vmem = pl.BlockSpec(memory_space=pltpu.VMEM)
    hbm = pl.BlockSpec(memory_space=pl.ANY)
    dma = pltpu.SemaphoreType.DMA
    copies = 2 * CHUNKS * 13 + 1 + 1 + 4 + GROUPS * 9
    return pl.pallas_call(
        kernel,
        out_shape=(
            jax.ShapeDtypeStruct((LAT, COLS), BF16),
            jax.ShapeDtypeStruct((ROWS, D), BF16),
        ),
        in_specs=[vmem, hbm, hbm, vmem, vmem, vmem],
        out_specs=(vmem, vmem),
        scratch_shapes=[
            pltpu.VMEM((2, D, COLS), BF16),
            pltpu.VMEM((ROWS, D), BF16),
            pltpu.VMEM((2, NZ, NX, NY, LAT, COLS), BF16),
            pltpu.VMEM((2, 2, 2, ROWS, COLS), BF16),
            pltpu.VMEM((2, 8, BLOCK), F32),
            pltpu.VMEM((2, 2, 8, LATENTS), F32),
            pltpu.VMEM((STEPS, 8, TILE), F32),
            pltpu.VMEM((PEERS, 8, TILE), F32),
            pltpu.VMEM((STEPS, 8, TILE), F32),
            pltpu.VMEM((2 * ROWS, LATENTS), BF16),
            pltpu.VMEM((2 * ROWS, LATENTS), BF16),
            pltpu.VMEM((HEADS, NZ, NX, NY, LAT, HEAD_DIM), F32),
            pltpu.VMEM((GROUPS, 2, size, 4, LAT, HEAD_DIM), F32),
            pltpu.VMEM((GROUPS, 2, size, NZ, 4, LAT, HEAD_DIM), F32),
            pltpu.VMEM((GROUPS, 2, size, LAT, HEAD_DIM), F32),
            pltpu.VMEM((GROUPS, 2, size, NZ, LAT, HEAD_DIM), F32),
            pltpu.VMEM((GROUPS, size, LAT, HEAD_DIM), F32),
            pltpu.VMEM((2, 2, 2, ROWS, COLS), F32),
            pltpu.VMEM((2, 2, ROWS, COLS), F32),
            pltpu.VMEM((2, ROWS, COLS), BF16),
            pltpu.VMEM((ROWS, D), F32),
            pltpu.VMEM((ROWS, D), F32),
            dma((2,)),
            dma((2 * CHUNKS,)),
            dma((copies,)),
            dma((copies,)),
            dma((STEPS,)),
            dma((PEERS,)),
            dma((PEERS,)),
            dma((PEERS,)),
            dma((2, HEADS)),
            dma((2, HEADS)),
            dma((D // 256,)),
            dma((D // 256,)),
        ],
        compiler_params=pltpu.CompilerParams(
            collective_id=0, has_side_effects=True, vmem_limit_bytes=60 << 20
        ),
        cost_estimate=pl.CostEstimate(
            flops=20_000_000_000, bytes_accessed=12 << 20, transcendentals=13_000_000
        ),
        name="attention_backward",
    )(prefix, w_key, w_value, queries, output_grad, mask)


def solution(mesh):
    return jax.shard_map(
        local,
        mesh=mesh,
        in_specs=(
            P(("blk", "head"), None),
            P(None, "head"),
            P(None, "head"),
            P("blk", "head"),
            P("blk", "head"),
            P(None, "blk"),
        ),
        out_specs=(P("blk", "head"), P(("blk", "head"), None)),
        check_vma=False,
    )
```

time: 1170 us -> 158 us (0.14)
  waiting for transfers between devices: 881 us -> 0 us
  Pallas kernels: 0 us -> 152 us
  other arithmetic: 129 us -> 0.68 us
  matrix products: 78 us -> 0 us
  local copies, waits for them, and re-layouts: 61.2 us -> 4.38 us
  between operations: 14.3 us -> 0.65 us
    all_gather x6 -> x0, waiting for transfers between devices: 543 us -> none  [the longest x3 316 us: combined_all(): gathered = jax.tree.map(lambda a: lax.all_gather(a, axis), part)]
    reduce_scatter x2 -> x0, waiting for transfers between devices: 334 us -> none  [the longest x1 297 us: local(): lax.psum_scatter(query_sum.reshape(latents, head_cols), 'blk', scatter_di...]
    pallas_call x0 -> x1, Pallas kernels: none -> 152 us  [local(): pl.pallas_call(kernel, out_shape=(jax.ShapeDtypeStruct((LAT, COLS), BF16)...]
    add x126 -> x0, other arithmetic: 116 us -> none  [the longest x63 58.4 us: join_stats(): left[1] * left_factor + right[1] * right_factor]
    dot_general x32 -> x0, matrix products: 78 us -> none  [the longest x8 19.1 us: score_block(): jnp.einsum('igd,pgd->gip', query_rows, key_block, preferred_element_type=...]
    unnamed x18 -> x2, local copies, waits for them, and re-layouts: 17.6 us -> 3.56 us
    all_gather x2 -> x0, local copies, waits for them, and re-layouts: 13.1 us -> none  [the longest x1 6.57 us: local(): lax.all_gather(output_grad, 'blk', axis=0, tiled=True)]
  transfers between devices with their start and end apart: 8 -> 0, of which waited for: 8 -> 0; matrix products, arithmetic and copies ran while one was open for 3% -> 0% of each run, Pallas kernels for 0% -> 0%
where the time goes in v1:
time: 158 us
  Pallas kernels  152 us (96%)
  local copies, waits for them, and re-layouts  4.38 us (3%)
    pallas_call x1, Pallas kernels, local(): pl.pallas_call(kernel, out_shape=(jax.ShapeDtypeStruct((LAT, COLS), BF16)...  152 us
    unnamed x2, local copies, waits for them, and re-layouts  3.56 us

profile of v1, /device:TPU:0, one launch (start us, length us, event | category | flops | bytes accessed | tf_op | source)
XLA Modules:
  0.0 158.0 jit_solution(3344912752628821417)
XLA Ops:
  0.6 0.7 compare_convert_fusion
  1.3 0.1 reshape.9
  1.4 0.1 copy.9
  1.5 0.6 pad.4.mask
  2.1 152.3 %attention_backward.1 = (bf16[32,1024]{1,0:T(8,128)(2,1)}, bf16[192,2048]{1,0:T(8,128)(2,1)}) custom-call(bf16[192,2048]{1,0:T(8,128)(2,1)} %prefix.1, bf16[2048,1024]{1,0:T(8,128)(2,1)} %w_key.1, bf16[2048,1024]{1,0:T(8,128)(2,1)} %w_value.1, bf16[32,1024]{1,0:T(8,128)(2,1)} %queries.1, bf16[32,1024]{1,0:T(8,128)(2,1)} %grads.1, f32[2,2,8,128]{3,2,1,0:T(8,128)} %pad.4.mask), custom_call_target="tpu_custom_call" | custom-call | flops 20000000000 | bytes 12582912 | tf_op jit(solution)/shard_map/attention_backward/pallas_call | solution.py:493
  154.4 1.5 copy.13
  155.9 2.1 %copy.14 = bf16[192,2048]{1,0:T(8,128)(2,1)} copy(bf16[192,2048]{1,0:T(8,128)(2,1)} %get-tuple-element.5) | data formatting | bytes 1572864
  (2 shorter events, 0.0 us)

commit v2 on v1

--- a/solution.py
+++ b/solution.py
@@ -26,9 +26,9 @@
 TILE = 256
 TILES = LATENTS // TILE
 STEPS = HEADS * TILES
-LAG = 4
+LAG = 16
 CHUNKS = 2
-GROUPS = 4
+PAD = 16
 SCALE = 1.0 / math.sqrt(HEAD_DIM)
 SCALE2 = SCALE * math.log2(math.e)
 NT = (((1,), (1,)), ((), ()))
@@ -40,6 +40,26 @@
     return lax.dot_general(a, b, dims, preferred_element_type=F32)
 
 
+def encode(value):
+    top = jnp.max(jnp.abs(value), axis=0, keepdims=True)
+    power = jnp.floor(jnp.log2(top + 1e-30) * 64.0) + 2.0
+    whole = jnp.round(value * (jnp.exp2(power * (-1.0 / 64.0)) * 32767.0))
+    powers = jnp.broadcast_to(power, (PAD, value.shape[1]))
+    return whole.astype(jnp.int32).astype(jnp.int16), powers.astype(jnp.int32).astype(jnp.int16)
+
+
+def put(ref, value):
+    rows = value.shape[0]
+    ref[0:rows], ref[rows : rows + PAD] = encode(value)
+
+
+def decode(ref, rows):
+    power = ref[rows : rows + PAD].astype(jnp.int32).astype(F32)[0:1]
+    return ref[0:rows].astype(jnp.int32).astype(F32) * (
+        jnp.exp2(power * (1.0 / 64.0)) * (1.0 / 32767.0)
+    )
+
+
 def lanes(index, width):
     return pl.ds(pl.multiple_of(index * width, width), width)
 
@@ -47,8 +67,8 @@
 def kernel(
     prefix, w_key, w_value, queries, grads, mask,
     dq_out, pg_out,
-    w, pref, gat, kv, mask_in, bias, stat, stat_in, glob, p_low, s_low, dq, r1, r2, r3, r4, r5,
-    dkv, dkv_in, low, back, back_in,
+    w, pref, gat, kv, mask_in, bias, stat, stat_in, glob, p_low, s_low, dq,
+    e1, e2, e3, e4, e5, r1, r2, r3, r4, r5, dkv, dkv_in, low, back, back_out, back_in,
     w_sem, own_sem, send_sem, recv_sem, stat_send, stat_recv, glob_send, glob_recv,
     dkv_send, dkv_recv, back_send, back_recv,
 ):
@@ -97,16 +117,24 @@
 
     def send(src, dst, device):
         index = len(used)
-        copy = pltpu.make_async_remote_copy(
-            src_ref=src, dst_ref=dst, send_sem=send_sem.at[index], recv_sem=recv_sem.at[index],
-            device_id=device, device_id_type=MESH,
-        )
-        copy.start()
+
+        def view(place):
+            return place[0].at[place[1:]] if isinstance(place, tuple) else place
+
+        def copy():
+            return pltpu.make_async_remote_copy(
+                src_ref=view(src), dst_ref=view(dst),
+                send_sem=send_sem.at[index], recv_sem=recv_sem.at[index],
+                device_id=device, device_id_type=MESH,
+            )
+
+        copy().start()
         used.append(copy)
         return copy
 
     shards = (queries, grads)
-    rings = (((xp, xm, x, x1, x3), (yp, ym, y, y1, y3)), ((yp, ym, y, y1, y3), (xp, xm, x, x1, x3)))
+    along_x, along_y = (xp, xm, x, x1, x2, x3), (yp, ym, y, y1, y2, y3)
+    rings = ((along_x, along_y), (along_y, along_x))
 
     def block(t, z_, first, second, cols):
         if t == 0:
@@ -124,7 +152,7 @@
     def relay(c, step):
         cols = pl.ds(c * width, width)
         for t in range(2):
-            (p1, m1, a, a_up, a_dn), (p2, m2, e, e_up, e_dn) = rings[t]
+            (p1, m1, a, a_up, _, a_dn), (p2, m2, e, e_up, _, e_dn) = rings[t]
             key = (c, t)
             if step == 0:
                 mine = shards[t].at[:, cols]
@@ -133,35 +161,35 @@
                 own.start()
                 flight[key] = [send(mine, dst, zn), send(mine, dst, p1), send(mine, dst, m1), own]
             elif step == 1:
-                flight[key][0].wait_recv()
+                flight[key][0]().wait_recv()
                 src = block(t, 1 - z, a, e, cols)
                 flight[key] += [send(src, src, p1), send(src, src, m1)]
             elif step == 2:
                 for k in (1, 2, 4, 5):
-                    flight[key][k].wait_recv()
+                    flight[key][k]().wait_recv()
                 flight[key][3].wait()
                 lo, hi = block(t, 0, a_dn, e, cols), block(t, 1, a_up, e, cols)
                 flight[key] = [send(lo, lo, p1), send(hi, hi, m1)]
             elif step == 3:
                 for k in (0, 1):
-                    flight[key][k].wait_recv()
+                    flight[key][k]().wait_recv()
                 flight[key] = []
                 for z_ in range(NZ):
                     src = line(t, z_, e, cols)
                     flight[key] += [send(src, src, p2), send(src, src, m2)]
             elif step == 4:
                 for k in range(4):
-                    flight[key][k].wait_recv()
+                    flight[key][k]().wait_recv()
                 lo, hi = line(t, 0, e_dn, cols), line(t, 1, e_up, cols)
                 flight[key] = [send(lo, lo, p2), send(hi, hi, m2)]
             else:
                 for k in (0, 1):
-                    flight[key][k].wait_recv()
+                    flight[key][k]().wait_recv()
 
     for c in range(CHUNKS):
         relay(c, 0)
     pref_copy = send(prefix, pref, partner)
-    mask_copy = send(mask.at[1 - core], mask_in, sibling)
+    mask_copy = send(mask, mask_in, sibling)
 
     def project(rows, half):
         def column(j, carry):
@@ -181,28 +209,29 @@
     relay(0, 2)
     relay(1, 2)
 
-    which = lax.broadcasted_iota(jnp.int32, (BLOCK, LATENTS), 0)
-    latent = lax.broadcasted_iota(jnp.int32, (BLOCK, LATENTS), 1)
-    spread = jnp.where(lax.div(latent, LAT) == which, 1.0, 0.0).astype(BF16)
+    group = lax.broadcasted_iota(jnp.int32, (2 * PEERS, LATENTS), 0)
+    latent = lax.broadcasted_iota(jnp.int32, (2 * PEERS, LATENTS), 1)
+    spread = jnp.where(2 * lax.div(latent, LAT) + core == group, 1.0, 0.0).astype(BF16)
 
     def fill_bias(row_core, source):
-        for half in range(2):
-            live = dot(source[half].astype(BF16), spread, NN)
-            bias[row_core, half] = jnp.where(live > 0.5, 0.0, FILL)
-
-    fill_bias(core, mask[core])
-    mask_copy.wait_recv()
-    fill_bias(1 - core, mask_in[...])
+        live = dot(jnp.where(source[...] != 0, 1.0, 0.0).astype(BF16), spread, TN)
+        for unit in range(2 * ROWS // UNIT):
+            row = live[unit * UNIT // BLOCK : unit * UNIT // BLOCK + 1]
+            bias[row_core, unit // 3, unit % 3 : unit % 3 + 1, :] = jnp.where(row > 0.5, 0.0, FILL)
+
+    fill_bias(core, mask)
+    mask_copy().wait_recv()
+    fill_bias(1 - core, mask_in)
     relay(0, 3)
     relay(1, 3)
-    pref_copy.wait_recv()
+    pref_copy().wait_recv()
     kv_copies += project(pref, 1 - head)
     relay(0, 4)
     relay(1, 4)
     relay(0, 5)
     relay(1, 5)
     for copy in kv_copies:
-        copy.wait_recv()
+        copy().wait_recv()
 
     def stat_copy(step):
         return pltpu.make_async_remote_copy(
@@ -368,9 +397,8 @@
         return dot(low[0], w[0, rows, :], NT) + dot(low[1], w[1, rows, :], NT)
 
     def back_copy(j):
-        cols = lanes(j, 256)
         return pltpu.make_async_remote_copy(
-            src_ref=back.at[:, cols], dst_ref=back_in.at[:, cols],
+            src_ref=back_out.at[j], dst_ref=back_in.at[j],
             send_sem=back_send.at[j], recv_sem=back_recv.at[j],
             device_id=partner, device_id_type=MESH,
         )
@@ -379,91 +407,111 @@
         backward(0, 1 - head, h)
         return carry
 
-    def second_part(h, carry):
-        backward(1, head, h)
-        return carry
-
     lax.fori_loop(0, HEADS, first_part, 0)
     lower(0)
 
     def back_send_out(j, carry):
+        put(back_out.at[j], back_product(j))
+        back_copy(j).start()
+        return carry
+
+    lax.fori_loop(0, D // 256, back_send_out, 0)
+
+    ahead = {}
+    cell_rows = LAT
+    line_rows = 4 * LAT
+
+    def reduce(h, step):
+        (p1, m1, a, a1, a2, a3), (p2, m2, f, f1, f2, f3) = rings[1 - h % 2]
+
+        def line_ref(z_, k):
+            return dq.at[h, z_, :, k] if h % 2 == 0 else dq.at[h, z_, k]
+
+        def line_of(z_, k):
+            return line_ref(z_, k)[...].reshape(line_rows, HEAD_DIM)
+
+        def cell_ref(z_, k):
+            return dq.at[h, z_, k, a] if h % 2 == 0 else dq.at[h, z_, a, k]
+
+        for copy in ahead.get(h, ()):
+            copy().wait_recv()
+        if step == 0:
+            put(e1.at[h, 0], line_of(0, a2))
+            put(e1.at[h, 1], line_of(1, a2))
+            ahead[h] = [send((e1, h, 0), (r1, h, 0), p1), send((e1, h, 1), (r1, h, 1), m1)]
+        elif step == 1:
+            put(e2.at[h, 0, 0], line_of(0, a1) + decode(r1.at[h, 0], line_rows))
+            put(e2.at[h, 0, 1], line_of(1, a1))
+            put(e2.at[h, 1, 0], line_of(0, a3))
+            put(e2.at[h, 1, 1], line_of(1, a3) + decode(r1.at[h, 1], line_rows))
+            ahead[h] = [send((e2, h, 0), (r2, h, 0), p1), send((e2, h, 1), (r2, h, 1), m1)]
+        elif step == 2:
+            for z_ in range(NZ):
+                total = line_of(z_, a)
+                for k in range(2):
+                    total += decode(r2.at[h, k, z_], line_rows)
+                line_ref(z_, a)[...] = total.reshape(4, LAT, HEAD_DIM)
+            put(e3.at[h, 0], cell_ref(0, f2)[...])
+            put(e3.at[h, 1], cell_ref(1, f2)[...])
+            ahead[h] = [send((e3, h, 0), (r3, h, 0), p2), send((e3, h, 1), (r3, h, 1), m2)]
+        elif step == 3:
+            put(e4.at[h, 0, 0], cell_ref(0, f1)[...] + decode(r3.at[h, 0], cell_rows))
+            put(e4.at[h, 0, 1], cell_ref(1, f1)[...])
+            put(e4.at[h, 1, 0], cell_ref(0, f3)[...])
+            put(e4.at[h, 1, 1], cell_ref(1, f3)[...] + decode(r3.at[h, 1], cell_rows))
+            ahead[h] = [send((e4, h, 0), (r4, h, 0), p2), send((e4, h, 1), (r4, h, 1), m2)]
+        elif step == 4:
+            for z_ in range(NZ):
+                total = cell_ref(z_, f)[...]
+                for k in range(2):
+                    total += decode(r4.at[h, k, z_], cell_rows)
+                cell_ref(z_, f)[...] = total
+            put(e5.at[h], cell_ref(1 - z, f)[...])
+            ahead[h] = [send((e5, h), (r5, h), zn)]
+        else:
+            result = cell_ref(z, f)[...] + decode(r5.at[h], cell_rows)
+            dq_out[:, h * HEAD_DIM : (h + 1) * HEAD_DIM] = (result * SCALE).astype(BF16)
+
+    pairs = HEADS // 2
+
+    def wave(index):
+        for p in range(pairs):
+            if 0 <= index - p < 6:
+                reduce(2 * p, index - p)
+                reduce(2 * p + 1, index - p)
+
+    def second_waves(h, carry):
+        backward(1, head, h)
+        for p in range(pairs):
+
+            @pl.when(h == 2 * p + 1)
+            def _():
+                wave(p)
+
+        return carry
+
+    lax.fori_loop(0, HEADS, second_waves, 0)
+
+    def own_product(j, carry):
         back[:, lanes(j, 256)] = back_product(j)
-        back_copy(j).start()
-        return carry
-
-    lax.fori_loop(0, D // 256, back_send_out, 0)
-    lax.fori_loop(0, HEADS, second_part, 0)
-
-    size = HEADS // GROUPS
-    ahead = {}
-
-    def reduce(g, step):
-        hs = pl.ds(g * size, size)
-        first, second = rings[1 - g % 2]
-        (p1, m1, a, a1, a3), (p2, m2, e, e1, e3) = first, second
-        a2, e2 = up(a, 2), up(e, 2)
-
-        def plane(z_, k):
-            return dq.at[hs, z_, :, k] if g % 2 == 0 else dq.at[hs, z_, k]
-
-        def planes(k):
-            return dq.at[hs, :, :, k] if g % 2 == 0 else dq.at[hs, :, k]
-
-        def cell(z_, k):
-            return dq.at[hs, z_, k, a] if g % 2 == 0 else dq.at[hs, z_, a, k]
-
-        def cells(k):
-            return dq.at[hs, :, k, a] if g % 2 == 0 else dq.at[hs, :, a, k]
-
-        def add(ref, *terms):
-            value = ref[...]
-            for term in terms:
-                value = value + term
-            ref[...] = value
-
-        if step == 0:
-            ahead[g] = [send(plane(0, a2), r1.at[g, 0], p1), send(plane(1, a2), r1.at[g, 1], m1)]
-            return
-        for copy in ahead[g]:
-            copy.wait_recv()
-        if step == 1:
-            add(plane(0, a1), r1[g, 0])
-            add(plane(1, a3), r1[g, 1])
-            ahead[g] = [send(planes(a1), r2.at[g, 0], p1), send(planes(a3), r2.at[g, 1], m1)]
-        elif step == 2:
-            add(planes(a), r2[g, 0], r2[g, 1])
-            ahead[g] = [send(cell(0, e2), r3.at[g, 0], p2), send(cell(1, e2), r3.at[g, 1], m2)]
-        elif step == 3:
-            add(cell(0, e1), r3[g, 0])
-            add(cell(1, e3), r3[g, 1])
-            ahead[g] = [send(cells(e1), r4.at[g, 0], p2), send(cells(e3), r4.at[g, 1], m2)]
-        elif step == 4:
-            add(cells(e), r4[g, 0], r4[g, 1])
-            ahead[g] = [send(dq.at[hs, 1 - z, x, y], r5.at[g], zn)]
-        else:
-            result = ((dq[hs, z, x, y] + r5[g]) * SCALE).astype(BF16)
-            for k in range(size):
-                dq_out[:, pl.ds((g * size + k) * HEAD_DIM, HEAD_DIM)] = result[k]
-
-    pairs = GROUPS // 2
-    for wave in range(6 + pairs - 1):
-        for g in range(GROUPS):
-            if 0 <= wave - g // 2 < 6:
-                reduce(g, wave - g // 2)
-
+        return carry
+
+    wave(pairs)
     lower(1)
+    lax.fori_loop(0, D // 256, own_product, 0)
+    for index in range(pairs + 1, pairs + 5):
+        wave(index)
 
     def finish(j, carry):
         cols = lanes(j, 256)
-        mine = back_product(j)
         back_copy(j).wait_recv()
-        pg_out[:, cols] = (mine + back_in[:, cols]).astype(BF16)
+        pg_out[:, cols] = (back[:, cols] + decode(back_in.at[j], ROWS)).astype(BF16)
         return carry
 
     lax.fori_loop(0, D // 256, finish, 0)
 
     for copy in used:
-        copy.wait_send()
+        copy().wait_send()
 
     def settle(k, carry):
         stat_copy(lax.rem(me + k, PEERS)).wait_send()
@@ -482,14 +530,18 @@
 
 
 def local(prefix, w_key, w_value, queries, output_grad, block_mask):
-    live = (block_mask != 0).astype(F32).reshape(PEERS, 2, 3).transpose(1, 2, 0)
-    units = jnp.repeat(live, BLOCK // UNIT, axis=1).reshape(2, 2, 3, PEERS)
-    mask = jnp.pad(units, ((0, 0), (0, 0), (0, 5), (0, BLOCK - PEERS)))
-    size = HEADS // GROUPS
     vmem = pl.BlockSpec(memory_space=pltpu.VMEM)
     hbm = pl.BlockSpec(memory_space=pl.ANY)
     dma = pltpu.SemaphoreType.DMA
-    copies = 2 * CHUNKS * 13 + 1 + 1 + 4 + GROUPS * 9
+    copies = 2 * CHUNKS * 13 + 1 + 1 + 4 + HEADS * 9
+    line, cell = 4 * LAT + PAD, LAT + PAD
+    coded = [
+        pltpu.VMEM((HEADS, 2, line, HEAD_DIM), jnp.int16),
+        pltpu.VMEM((HEADS, 2, NZ, line, HEAD_DIM), jnp.int16),
+        pltpu.VMEM((HEADS, 2, cell, HEAD_DIM), jnp.int16),
+        pltpu.VMEM((HEADS, 2, NZ, cell, HEAD_DIM), jnp.int16),
+        pltpu.VMEM((HEADS, cell, HEAD_DIM), jnp.int16),
+    ]
     return pl.pallas_call(
         kernel,
         out_shape=(
@@ -503,7 +555,7 @@
             pltpu.VMEM((ROWS, D), BF16),
             pltpu.VMEM((2, NZ, NX, NY, LAT, COLS), BF16),
             pltpu.VMEM((2, 2, 2, ROWS, COLS), BF16),
-            pltpu.VMEM((2, 8, BLOCK), F32),
+            pltpu.VMEM((2 * PEERS, 3), jnp.int32),
             pltpu.VMEM((2, 2, 8, LATENTS), F32),
             pltpu.VMEM((STEPS, 8, TILE), F32),
             pltpu.VMEM((PEERS, 8, TILE), F32),
@@ -511,16 +563,14 @@
             pltpu.VMEM((2 * ROWS, LATENTS), BF16),
             pltpu.VMEM((2 * ROWS, LATENTS), BF16),
             pltpu.VMEM((HEADS, NZ, NX, NY, LAT, HEAD_DIM), F32),
-            pltpu.VMEM((GROUPS, 2, size, 4, LAT, HEAD_DIM), F32),
-            pltpu.VMEM((GROUPS, 2, size, NZ, 4, LAT, HEAD_DIM), F32),
-            pltpu.VMEM((GROUPS, 2, size, LAT, HEAD_DIM), F32),
-            pltpu.VMEM((GROUPS, 2, size, NZ, LAT, HEAD_DIM), F32),
-            pltpu.VMEM((GROUPS, size, LAT, HEAD_DIM), F32),
+            *coded,
+            *coded,
             pltpu.VMEM((2, 2, 2, ROWS, COLS), F32),
             pltpu.VMEM((2, 2, ROWS, COLS), F32),
             pltpu.VMEM((2, ROWS, COLS), BF16),
             pltpu.VMEM((ROWS, D), F32),
-            pltpu.VMEM((ROWS, D), F32),
+            pltpu.VMEM((D // 256, ROWS + PAD, 256), jnp.int16),
+            pltpu.VMEM((D // 256, ROWS + PAD, 256), jnp.int16),
             dma((2,)),
             dma((2 * CHUNKS,)),
             dma((copies,)),
@@ -541,7 +591,7 @@
             flops=20_000_000_000, bytes_accessed=12 << 20, transcendentals=13_000_000
         ),
         name="attention_backward",
-    )(prefix, w_key, w_value, queries, output_grad, mask)
+    )(prefix, w_key, w_value, queries, output_grad, block_mask)
 
 
 def solution(mesh):

time: 158 us -> 128 us (0.81)
  Pallas kernels: 152 us -> 122 us
    pallas_call x1, Pallas kernels: 152 us -> 122 us  [local(): pl.pallas_call(kernel, out_shape=(jax.ShapeDtypeStruct((LAT, COLS), BF16)...]
    unnamed x2 -> x3, local copies, waits for them, and re-layouts: 3.56 us -> 4.95 us
where the time goes in v2:
time: 128 us
  Pallas kernels  122 us (95%)
  local copies, waits for them, and re-layouts  4.95 us (4%)
    pallas_call x1, Pallas kernels, local(): pl.pallas_call(kernel, out_shape=(jax.ShapeDtypeStruct((LAT, COLS), BF16)...  122 us
    unnamed x3, local copies, waits for them, and re-layouts  4.95 us

profile of v2, /device:TPU:0, one launch (start us, length us, event | category | flops | bytes accessed | tf_op | source)
XLA Modules:
  0.0 127.7 jit_solution(10578910858314397897)
XLA Ops:
  0.6 1.4 %copy.8.mask = s32[64,3]{1,0:T(8,128)} copy(s32[64,3]{0,1:T(4,128)} %param.11) | data formatting | bytes 1536 | tf_op args[5]
  2.0 122.1 %attention_backward.1 = (bf16[32,1024]{1,0:T(8,128)(2,1)}, bf16[192,2048]{1,0:T(8,128)(2,1)}) custom-call(bf16[192,2048]{1,0:T(8,128)(2,1)} %prefix.1, bf16[2048,1024]{1,0:T(8,128)(2,1)} %w_key.1, bf16[2048,1024]{1,0:T(8,128)(2,1)} %w_value.1, bf16[32,1024]{1,0:T(8,128)(2,1)} %queries.1, bf16[32,1024]{1,0:T(8,128)(2,1)} %grads.1, s32[64,3]{1,0:T(8,128)} %copy.8.mask), custom_call_target="tpu_custom_call" | custom-call | flops 20000000000 | bytes 12582912 | tf_op jit(solution)/shard_map/attention_backward/pallas_call | solution.py:545
  124.1 1.5 %copy.11 = bf16[32,1024]{1,0:T(8,128)(2,1)} copy(bf16[32,1024]{1,0:T(8,128)(2,1)} %get-tuple-element.4) | data formatting | bytes 131072
  125.6 2.1 %copy.12 = bf16[192,2048]{1,0:T(8,128)(2,1)} copy(bf16[192,2048]{1,0:T(8,128)(2,1)} %get-tuple-element.5) | data formatting | bytes 1572864
